TPU v7x, 1024 devices: a whole 8x8x8 slice. The times are simulated.
1024 devices in a mesh: node: 128 (over x, z, core), chip: 8 (over y).
Axes of the slice: x: 8, y: 8, z: 8, core: 2. Of those that a mesh axis runs over, the one named last changes fastest.
Arguments:
- grad_out: bfloat16 [4096, 4096], P('node', 'chip'), may hold values from -6 to 6
- route_score: bfloat16 [4096, 8], P('node'), may hold values from 0.049804688 to 0.5
- expert_routes: int32 [256, 256], P('node'), may hold values from 0 to 32767, as said below
- expert_count: int32 [256], P('node'), may hold values from 0 to 256, as said below
- gate_pre: bfloat16 [256, 256, 1024], P('node', None, 'chip'), may hold values from -6 to 6
- up_pre: bfloat16 [256, 256, 1024], P('node', None, 'chip'), may hold values from -6 to 6
- w_down: bfloat16 [256, 1024, 4096], P('node', 'chip'), may hold values from -0.1875 to 0.1875
Outputs:
- grad_gate: bfloat16 [256, 256, 1024], P('node', None, 'chip')
- grad_up: bfloat16 [256, 256, 1024], P('node', None, 'chip')
- grad_score: float32 [4096, 8], P('node')
Inputs may be any that keep to these rules, and one draw needn't show every extreme that they name: `expert_routes`: the alive slots of an expert hold distinct routes in increasing order, and each route index stands in at most one alive slot; slots at or beyond expert_count hold 0. Each route names the expert that the token chose at that position; the 8 experts of a token are distinct and lie in at most 4 of the 8 groups of 32 consecutive experts. `expert_count`: some expert is full in every draw.
All inputs are finite; a program needn't handle non-finite values.
Results may differ from a plain program's by a relative error of at most 0.001.
Values may be sent and summed in bfloat16 or wider, within the bound.
A program may use at most 32 MiB of HBM per device.

v0:
```python
import jax
import jax.numpy as jnp
from jax import lax
from jax.sharding import PartitionSpec as P


def on_device(grad_out, route_score, expert_routes, expert_count, gate_pre, up_pre, w_down):
    top_count = route_score.shape[1]
    exp_count, cap_slots = expert_routes.shape
    slot_count = exp_count * cap_slots
    routes = expert_routes.reshape(slot_count)
    token_ids = routes // top_count
    positions = routes % top_count
    alive = (jnp.arange(cap_slots, dtype=jnp.int32)[None, :] < expert_count[:, None]).reshape(
        slot_count
    )
    total_tokens = grad_out.shape[0] * lax.axis_size("node")
    gathered_rows, gathered_scores = (
        lax.all_gather(grad_out, "node", axis=0, tiled=True),
        lax.all_gather(route_score, "node", axis=0, tiled=True),
    )
    picked = jnp.where(alive[:, None], gathered_rows[token_ids], jnp.zeros((), jnp.bfloat16))
    slot_weight = jnp.where(
        alive, gathered_scores[token_ids, positions].astype(jnp.float32), jnp.float32(0.0)
    )
    columns_piece = lax.all_gather(picked, "chip", axis=1, tiled=True)
    span_width = columns_piece.shape[1]
    rows_block = columns_piece.reshape(exp_count, cap_slots, span_width)
    back = jnp.einsum("ecd,efd->ecf", rows_block, w_down, preferred_element_type=jnp.float32)
    pre_gate = gate_pre.astype(jnp.float32)
    pre_up = up_pre.astype(jnp.float32)
    sigmoid_gate = jax.nn.sigmoid(pre_gate)
    silu_gate = pre_gate * sigmoid_gate
    hidden = silu_gate * pre_up
    partial_slot = jnp.sum(hidden * back, axis=2).reshape(slot_count)
    scaled_back = slot_weight.reshape(exp_count, cap_slots)[:, :, None] * back
    alive_mask = alive.reshape(exp_count, cap_slots)[:, :, None]
    derivative = sigmoid_gate * (1.0 + pre_gate * (1.0 - sigmoid_gate))
    grad_gate = jnp.where(alive_mask, scaled_back * pre_up * derivative, jnp.float32(0.0)).astype(
        jnp.bfloat16
    )
    grad_up = jnp.where(alive_mask, scaled_back * silu_gate, jnp.float32(0.0)).astype(jnp.bfloat16)
    slot_total = lax.psum(partial_slot, "chip")
    flat_term = jnp.zeros((total_tokens * top_count,), jnp.float32)
    flat_term = flat_term.at[routes].add(jnp.where(alive, slot_total, jnp.float32(0.0)))
    grad_score = lax.psum_scatter(
        flat_term.reshape(total_tokens, top_count), "node", scatter_dimension=0, tiled=True
    )
    return (grad_gate, grad_up, grad_score)


def solution(mesh):
    placed = (
        P("node", "chip"),
        P("node", None),
        P("node", None),
        P("node"),
        P("node", None, "chip"),
        P("node", None, "chip"),
        P("node", "chip", None),
    )
    return jax.shard_map(
        on_device,
        mesh=mesh,
        in_specs=placed,
        out_specs=(P("node", None, "chip"), P("node", None, "chip"), P("node", None)),
        check_vma=False,
    )
```

profile of v0, /device:TPU:1, one launch (start us, length us, event | category | flops | bytes accessed | tf_op | source)
XLA Modules:
  0.0 418.3 jit_solution(9825078149030084113)
XLA Ops:
  7.2 0.0 copy-start
  7.2 0.0 copy-start.3
  7.2 0.0 all-gather.4.cloned.1.call-start
  7.2 0.7 all-gather.4.cloned.1.call-update
  7.9 0.0 all-gather.6.cloned.1.call-start
  8.0 0.7 copy.33
  8.7 0.7 iota_compare_fusion
  9.5 0.0 copy-start.1
  9.5 0.0 copy-start.2
  9.5 0.0 copy-start.4
  9.5 107.2 %all-gather.4.cloned.1.call-done = bf16[4096,512]{1,0:T(8,128)(2,1)} async-done(((bf16[32,512]{1,0:T(8,128)(2,1)}), bf16[4096,512]{1,0:T(8,128)(2,1)}) %all-gather.4.cloned.1.call-update) | async-done | bytes 4194320 | tf_op jit(solution)/shard_map/all_gather | solution.py:19
  116.7 4.7 %gather_fusion.1 = bf16[512,512]{1,0:T(8,128)(2,1)S(1)} fusion(bf16[4096,512]{1,0:T(8,128)(2,1)} %all-gather.4.cloned.1.call-done, s32[1024]{0:T(1024)S(1)} %pad_clamp_fusion), kind=kCustom, calls=%fused_computation.1 | custom fusion | bytes 1050624 | tf_op jit(solution)/shard_map/gather | solution.py:22
  121.4 1.0 broadcast_select_fusion
  122.3 0.0 all-gather.6.cloned.1.call-update
  122.4 0.0 reduce-scatter.2.cloned.1.call-start
  122.4 0.0 copy-done.3
  122.4 48.5 %all-gather = bf16[128,32,8]{1,2,0:T(8,128)(2,1)S(1)} all-gather(bf16[1,32,8]{1,2,0:T(8,128)(2,1)S(1)} %bitcast.19), channel_id=1, replica_groups=mesh['node'=128,'chip'=8] {'node'}, dimensions={0}, use_global_device_ids=true | all-gather | bytes 66048 | tf_op jit(solution)/shard_map/all_gather | solution.py:20
  171.0 0.3 reshape.250
  171.2 4.6 %gather_fusion = bf16[512]{0:T(512)(128)(2,1)S(1)} fusion(bf16[4096,8]{0,1:T(8,128)(2,1)S(1)} %reshape.250, s32[512]{0:T(512)S(1)} %bitcast.15), kind=kCustom, calls=%fused_computation | custom fusion | bytes 6144 | tf_op jit(solution)/shard_map/gather | solution.py:24
  175.8 0.0 copy-done.1
  175.8 0.1 copy.28
  176.0 0.0 copy-done.2
  176.0 0.1 copy.29
  176.1 0.0 copy-done.4
  176.1 0.1 broadcast_select_fusion.2
  176.2 2.5 all-gather.6.cloned.1.call-done
  178.7 0.0 copy-done
  178.7 3.8 fusion.4
  182.5 12.0 %psum.7 = f32[512]{0:T(512)S(1)} all-reduce(f32[512]{0:T(512)S(1)} %bitcast.17), channel_id=1, replica_groups=mesh['node'=128,'chip'=8] {'chip'}, use_global_device_ids=true, to_apply=%region_1.2 | all-reduce | flops 512 | bytes 4096 | tf_op jit(solution)/shard_map/psum | solution.py:43
  194.5 4.1 scatter_custom_fusion
  198.6 2.5 reshape.225
  201.0 0.0 reduce-scatter.2.cloned.1.call-update
  201.1 0.8 copy.30
  201.8 0.8 copy.31
  202.6 207.9 %reduce-scatter.2.cloned.1.call-done = f32[32,8]{1,0:T(8,128)} async-done(((f32[4096,8]{1,0:T(8,128)}), f32[32,8]{1,0:T(8,128)}) %reduce-scatter.2.cloned.1.call-update) | async-done | bytes 1040 | tf_op jit(solution)/shard_map/reduce_scatter | solution.py:46
  410.4 1.4 copy.32
  (7 shorter events, 0.1 us)
Async XLA Ops:
  7.2 171.5 %copy-start = (bf16[2,128,4096]{2,1,0:T(8,128)(2,1)S(1)}, bf16[2,128,4096]{2,1,0:T(8,128)(2,1)}, u32[]{:S(2)}) copy-start(bf16[2,128,4096]{2,1,0:T(8,128)(2,1)} %param.13) | copy-start | bytes 6291460
  7.2 115.2 %copy-start.3 = (bf16[32,8]{0,1:T(8,128)(2,1)S(1)}, bf16[32,8]{0,1:T(8,128)(2,1)}, u32[]{:S(2)}) copy-start(bf16[32,8]{0,1:T(8,128)(2,1)} %param.8) | copy-start | bytes 1540
  7.2 109.5 %all-gather.4.cloned.1.call-start = ((), (), s32[]{:S(2)}) async-start(), calls=%async_computation.1 | async-start | bytes 4227072 | tf_op jit(solution)/shard_map/all_gather | solution.py:19
  7.9 170.8 %all-gather.6.cloned.1.call-start = ((), (), s32[]{:S(2)}) async-start(), calls=%async_computation.2 | async-start | bytes 4718592 | tf_op jit(solution)/shard_map/all_gather | solution.py:26
  9.5 166.4 %copy-start.1 = (bf16[2,256,128]{2,1,0:T(8,128)(2,1)S(1)}, bf16[2,256,128]{2,1,0:T(8,128)(2,1)}, u32[]{:S(2)}) copy-start(bf16[2,256,128]{2,1,0:T(8,128)(2,1)} %param.12) | copy-start | bytes 393220
  9.5 166.5 %copy-start.2 = (bf16[2,256,128]{2,1,0:T(8,128)(2,1)S(1)}, bf16[2,256,128]{2,1,0:T(8,128)(2,1)}, u32[]{:S(2)}) copy-start(bf16[2,256,128]{2,1,0:T(8,128)(2,1)} %param.11) | copy-start | bytes 393220
  9.5 166.6 %copy-start.4 = (s32[2]{0:T(128)S(1)}, s32[2]{0:T(128)}, u32[]{:S(2)}) copy-start(s32[2]{0:T(128)} %param.10) | copy-start | bytes 28
  122.4 288.1 %reduce-scatter.2.cloned.1.call-start = ((), (), s32[]{:S(2)}) async-start(), calls=%async_computation.3 | async-start | bytes 2113536 | tf_op jit(solution)/shard_map/reduce_scatter | solution.py:46
Sparse Core Ops, SparseCore 0:
  12.3 104.3 all-gather.3
  122.5 56.1 all-gather.5
  201.2 209.2 reduce-scatter.1
where the time goes:
time: 422 us; the launch traced here: 418 us
  waiting for transfers between devices  318 us (75%)
  blocking collectives  60.5 us (14%)
  local copies, waits for them, and re-layouts  15.9 us (4%)
  between operations  13.9 us (3%)
  other arithmetic  5.87 us (1%)
    reduce_scatter x1, waiting for transfers between devices, on_device(): lax.psum_scatter(flat_term.reshape(total_tokens, top_count), 'node', scat...  208 us
    all_gather x1, waiting for transfers between devices, on_device(): lax.all_gather(grad_out, 'node', axis=0, tiled=True)  107 us
    all_gather x1, blocking collectives, on_device(): lax.all_gather(route_score, 'node', axis=0, tiled=True)  48.5 us
    psum x1, blocking collectives, on_device(): slot_total = lax.psum(partial_slot, 'chip')  12 us
  transfers between devices with their start and end apart: 3, of which 3 were waited for; matrix products, arithmetic and copies ran while one was open for 2% of the time, Pallas kernels for 0%

commit v1 on v0

v1 whole, which is shorter than its diff:
```python
import functools

import jax
import jax.numpy as jnp
from jax import lax
from jax.experimental import pallas as pl
from jax.experimental.pallas import tpu as pltpu
from jax.sharding import PartitionSpec as P

LANES = 128
TOP_BITS = 3


def bits_of(size):
    return size.bit_length() - 1


def dot_f32(a, b):
    return jnp.dot(a, b, preferred_element_type=jnp.float32)


def remote(src, dst, send, recv, node, chip):
    return pltpu.make_async_remote_copy(
        src_ref=src,
        dst_ref=dst,
        send_sem=send,
        recv_sem=recv,
        device_id=(node, chip),
        device_id_type=pl.DeviceIdType.MESH,
    )


def kernel(
    n,
    ny,
    grad_ref,
    score_ref,
    routes_ref,
    count_ref,
    gate_hbm,
    up_hbm,
    w_hbm,
    grad_gate_ref,
    grad_up_ref,
    grad_score_ref,
    table,
    onehot,
    ids,
    pick_send,
    pick_recv,
    pick_own,
    picked,
    gate_buf,
    up_buf,
    w_buf,
    back,
    low_hot,
    sums,
    dense_send,
    dense_recv,
    total_buf,
    in_sem,
    ids_send_sem,
    ids_recv_sem,
    line_send,
    line_recv,
    ring_send,
    ring_recv,
    pick_send_sem,
    pick_recv_sem,
    chip_send,
    chip_recv,
    sum_send,
    sum_recv,
    dense_send_sem,
    dense_recv_sem,
    total_send,
    total_recv,
):
    chunks = table.shape[1]
    feats = chunks - 1
    tokens = table.shape[3]
    experts, cap = routes_ref.shape
    slots = experts * cap
    width = n * tokens
    half_ring, half_chip = n // 2, ny // 2
    nbits = bits_of(n)
    groups = ((0, 1), (1, chunks))

    node = lax.axis_index("node")
    chip = lax.axis_index("chip")
    core = lax.rem(node, 2)
    z = lax.rem(node // 2, n)
    x = node // (2 * n)
    line = x + core * (z - x)
    ring = z + core * (x - z)
    sibling = node + 1 - 2 * core

    def node_at(ring_pos, line_pos):
        at_x = line_pos + core * (ring_pos - line_pos)
        at_z = ring_pos + core * (line_pos - ring_pos)
        return (at_x * n + at_z) * 2 + core

    def line_peer(d):
        return lax.rem(line + d, n)

    loads = [
        pltpu.make_async_copy(w_hbm, w_buf, in_sem.at[0]),
        pltpu.make_async_copy(gate_hbm, gate_buf, in_sem.at[1]),
        pltpu.make_async_copy(up_hbm, up_buf, in_sem.at[2]),
    ]
    for load in loads:
        load.start()
    for f in range(feats):
        table[ring, f, line] = grad_ref[:, f * LANES : (f + 1) * LANES]
    padded = jnp.concatenate(
        [
            score_ref[...].astype(jnp.float32),
            jnp.zeros((tokens, LANES - score_ref.shape[1]), jnp.float32),
        ],
        axis=1,
    )
    table[ring, feats, line] = padded.astype(jnp.bfloat16)
    slot_lane = lax.broadcasted_iota(jnp.int32, (1, cap), 1)
    for e in range(experts):
        ids[0, e : e + 1, :] = jnp.where(
            slot_lane < count_ref[e], routes_ref[e : e + 1, :], -1
        )

    barrier = pltpu.get_barrier_semaphore()
    greeted = [(sibling, chip)]
    greeted += [(node_at(ring, line_peer(d)), chip) for d in range(1, n)]
    greeted += [(node_at(lax.rem(ring + d, n), line), chip) for d in sorted({1, n - 1})]
    greeted += [(node, lax.rem(chip + d, ny)) for d in range(1, ny)]
    for peer in greeted:
        pl.semaphore_signal(
            barrier, inc=1, device_id=peer, device_id_type=pl.DeviceIdType.MESH
        )
    pl.semaphore_wait(barrier, len(greeted))

    def ids_copy():
        return remote(ids.at[0], ids.at[1], ids_send_sem, ids_recv_sem, sibling, chip)

    def line_push(g, d):
        lo, hi = groups[g]
        block = table.at[ring, lo:hi, line]
        return remote(
            block, block, line_send.at[g, d], line_recv.at[g, line], node_at(ring, line_peer(d)), chip
        )

    def line_arrival(g, d):
        lo, hi = groups[g]
        peer = line_peer(d)
        block = table.at[ring, lo:hi, peer]
        return remote(
            block, block, line_send.at[g, d], line_recv.at[g, peer], node_at(ring, peer), chip
        )

    def ring_block(g, way, s, pos):
        lo, hi = groups[g]
        if s < half_ring:
            return table.at[pos, lo:hi]
        return table.at[pos, lo:hi, pl.ds(way * half_ring, half_ring)]

    def ring_copy(g, way, s, arrival):
        step = 1 if way == 0 else n - 1
        hop = s if arrival else s - 1
        pos = lax.rem(ring + (n - step) * hop, n)
        block = ring_block(g, way, s, pos)
        to = node_at(lax.rem(ring + step, n), line)
        return remote(block, block, ring_send.at[g, way, s - 1], ring_recv.at[g, way, s - 1], to, chip)

    def ring_start(g, s):
        for way in range(2):
            ring_copy(g, way, s, False).start()

    def ring_wait(g, s):
        for way in range(2):
            ring_copy(g, way, s, True).wait_recv()

    def chip_copy(f, way, s, arrival):
        step = 1 if way == 0 else ny - 1
        hop = s if arrival else s - 1
        pos = lax.rem(chip + (ny - step) * hop, ny)
        block = picked.at[pos, f] if s < half_chip else picked.at[pos, f, pl.ds(way * (experts // 2), experts // 2)]
        to = lax.rem(chip + step, ny)
        return remote(block, block, chip_send.at[f, way, s - 1], chip_recv.at[f, way, s - 1], node, to)

    def chip_start(f, s):
        for way in range(2):
            chip_copy(f, way, s, False).start()

    def chip_wait(f, s):
        for way in range(2):
            chip_copy(f, way, s, True).wait_recv()

    def pick_copy(f):
        return remote(
            pick_send.at[f], pick_recv.at[f], pick_send_sem.at[f], pick_recv_sem.at[f], sibling, chip
        )

    def build_onehot(side):
        lanes = min(width, LANES)
        for e in range(experts):
            for b in range(cap // LANES):
                row = ids[side, e : e + 1, b * LANES : (b + 1) * LANES]
                col = jnp.transpose(jnp.broadcast_to(row, (LANES, LANES)))[:, :lanes]
                col_node = col >> (TOP_BITS + bits_of(tokens))
                col_core = col_node & 1
                col_z = (col_node >> 1) & (n - 1)
                col_x = col_node >> (1 + nbits)
                col_line = col_x + core * (col_z - col_x)
                col_ring = col_z + core * (col_x - col_z)
                inner = (col >> TOP_BITS) & (tokens - 1)
                key = col_ring * width + col_line * tokens + inner
                key = jnp.where((col >= 0) & (col_core == core), key, -1)
                key = key - lax.broadcasted_iota(jnp.int32, (LANES, lanes), 1)
                first = (side * experts + e) * cap + b * LANES

                def body(p, carry):
                    for h in range(width // lanes):
                        hit = key == p * width + h * lanes
                        onehot[p, first : first + LANES, h * lanes : (h + 1) * lanes] = jnp.where(
                            hit, 1.0, 0.0
                        ).astype(jnp.bfloat16)
                    return carry

                lax.fori_loop(0, n, body, 0)

    def build_low_hot():
        lane = lax.broadcasted_iota(jnp.int32, (LANES, 2 * LANES), 1)
        for e in range(experts):
            for b in range(cap // LANES):
                row = ids[0, e : e + 1, b * LANES : (b + 1) * LANES]
                col = jnp.transpose(jnp.broadcast_to(row, (2 * LANES, LANES)))
                first = e * cap + b * LANES
                low_hot[first : first + LANES, :] = jnp.where(
                    (col & (2 * LANES - 1)) == lane, 1.0, 0.0
                ).astype(jnp.bfloat16)

    def select(lo, hi, side, out):
        def body(e, carry):
            first = pl.multiple_of((side * experts + e) * cap, cap)
            total = jnp.zeros((cap, (hi - lo) * LANES), jnp.float32)
            for p in range(n):
                parts = [table[p, f].reshape(width, LANES) for f in range(lo, hi)]
                rhs = parts[0] if len(parts) == 1 else jnp.concatenate(parts, axis=1)
                total += dot_f32(onehot[p, pl.ds(first, cap), :], rhs)
            for f in range(lo, hi):
                out[f, e] = total[:, (f - lo) * LANES : (f - lo + 1) * LANES].astype(jnp.bfloat16)
            return carry

        lax.fori_loop(0, experts, body, 0)

    def send_picks(lo, hi):
        select(lo, hi, 1, pick_send)
        for f in range(lo, hi):
            pick_copy(f).start()
        select(lo, hi, 0, pick_own)

    def merge(f):
        pick_copy(f).wait_recv()
        picked[chip, f] = pick_own[f] + pick_recv[f]

    def multiply(f, first):
        def body(e, carry):
            total = jnp.zeros((cap, LANES), jnp.float32) if first else back[e]
            for y in range(ny):
                col = (y * feats + f) * LANES
                total += lax.dot_general(
                    picked[y, f, e],
                    w_buf[e, :, col : col + LANES],
                    (((1,), (1,)), ((), ())),
                    preferred_element_type=jnp.float32,
                )
            back[e] = total
            return carry

        lax.fori_loop(0, experts, body, 0)

    ids_copy().start()
    for g in range(2):
        for d in range(1, n):
            line_push(g, d).start()
    build_onehot(0)
    for d in range(1, n):
        line_arrival(0, d).wait_recv()
    ring_start(0, 1)
    ids_copy().wait_recv()
    build_onehot(1)
    for s in range(1, half_ring):
        ring_wait(0, s)
        ring_start(0, s + 1)
    for d in range(1, n):
        line_arrival(1, d).wait_recv()
    ring_start(1, 1)
    ring_wait(0, half_ring)
    send_picks(0, 1)
    build_low_hot()
    merge(0)
    chip_start(0, 1)
    for load in loads:
        load.wait()
    for s in range(1, half_ring):
        ring_wait(1, s)
        ring_start(1, s + 1)
        if s < half_chip:
            chip_wait(0, s)
            chip_start(0, s + 1)
    ring_wait(1, half_ring)
    for lo in range(1, feats, 2):
        send_picks(lo, lo + 2)
        for f in range(lo, min(lo + 2, feats)):
            merge(f)
            chip_start(f, 1)
    for s in range(half_ring, half_chip):
        chip_wait(0, s)
        chip_start(0, s + 1)
    merge_scores = feats
    pick_copy(merge_scores).wait_recv()
    chip_wait(0, half_chip)
    multiply(0, True)
    for s in range(1, half_chip):
        for f in range(1, feats):
            chip_wait(f, s)
            chip_start(f, s + 1)
    for f in range(1, feats):
        chip_wait(f, half_chip)
        multiply(f, False)

    for e in range(experts):
        for b in range(cap // LANES):
            rows = slice(b * LANES, (b + 1) * LANES)
            g = gate_buf[e, rows, :].astype(jnp.float32)
            u = up_buf[e, rows, :].astype(jnp.float32)
            bk = back[e, rows, :]
            s = 1.0 / (1.0 + jnp.exp(-g))
            silu = g * s
            row = ids[0, e : e + 1, b * LANES : (b + 1) * LANES]
            place = jnp.transpose(jnp.broadcast_to(row, (LANES, LANES))) & ((1 << TOP_BITS) - 1)
            lane = lax.broadcasted_iota(jnp.int32, (LANES, LANES), 1)
            scores = pick_own[feats, e, rows, :].astype(jnp.float32) + pick_recv[
                feats, e, rows, :
            ].astype(jnp.float32)
            weight = jnp.sum(jnp.where(place == lane, scores, 0.0), axis=1, keepdims=True)
            product = silu * u * bk
            at = e * (cap // LANES) + b
            sums[chip, at : at + 1, :] = jnp.sum(jnp.transpose(product), axis=0, keepdims=True)
            scaled = weight * bk
            grad_gate_ref[e, rows, :] = (scaled * u * (s * (1.0 + g * (1.0 - s)))).astype(jnp.bfloat16)
            grad_up_ref[e, rows, :] = (scaled * silu).astype(jnp.bfloat16)

    def sum_copy(d, slot):
        return remote(
            sums.at[slot], sums.at[slot], sum_send.at[d], sum_recv.at[slot], node, lax.rem(chip + d, ny)
        )

    for d in range(1, ny):
        sum_copy(d, chip).start()
    for d in range(1, ny):
        sum_copy(d, lax.rem(chip + d, ny)).wait_recv()
    full = sums[0]
    for y in range(1, ny):
        full = full + sums[y]

    targets = 2 * n
    pieces = []
    for e in range(experts):
        for b in range(cap // LANES):
            at = e * (cap // LANES) + b
            row_node = ids[0, e : e + 1, b * LANES : (b + 1) * LANES] >> (TOP_BITS + bits_of(tokens))
            row_z = (row_node >> 1) & (n - 1)
            row_x = row_node >> (1 + nbits)
            row_target = jnp.where(
                ((row_z - row_x) & (n - 1)) == chip, row_x * 2 + (row_node & 1), -1
            )
            target = lax.broadcasted_iota(jnp.int32, (targets, LANES), 0)
            pieces.append(jnp.where(row_target == target, full[at : at + 1, :], 0.0))
    spread = jnp.concatenate(pieces, axis=1)
    high = spread.astype(jnp.bfloat16)
    rest = spread - high.astype(jnp.float32)
    middle = rest.astype(jnp.bfloat16)
    low = (rest - middle.astype(jnp.float32)).astype(jnp.bfloat16)
    dense = dot_f32(high, low_hot[...]) + dot_f32(middle, low_hot[...]) + dot_f32(low, low_hot[...])
    for i in range(targets):
        dense_send[i, 0:1, :] = dense[i : i + 1, :LANES]
        dense_send[i, 1:2, :] = dense[i : i + 1, LANES:]

    def dense_copy(i):
        at_x = i // 2
        at_z = lax.rem(at_x + chip, n)
        to = (at_x * n + at_z) * 2 + lax.rem(i, 2)
        return to, remote(
            dense_send.at[i], dense_recv.at[node], dense_send_sem.at[i], dense_recv_sem, to, chip
        )

    def dense_start(i, carry):
        to, copy = dense_copy(i)

        @pl.when(to != node)
        def _():
            copy.start()

        return carry

    lax.fori_loop(0, targets, dense_start, 0)
    owner = lax.rem(z - x + n, n) == chip

    def total_copy(d):
        return remote(
            total_buf, total_buf, total_send.at[d], total_recv, node, lax.rem(chip + d, ny)
        )

    @pl.when(owner)
    def _():
        dense_recv[node] = dense_send[2 * x + core]
        others = dense_recv.at[pl.ds(0, dense_recv.shape[0] - 1)]
        pltpu.make_async_copy(others, others, dense_recv_sem).wait()
        total_buf[...] = jnp.sum(dense_recv[...], axis=0)
        for d in range(1, ny):
            total_copy(d).start()
        for d in range(1, ny):
            total_copy(d).wait_send()

    @pl.when(jnp.logical_not(owner))
    def _():
        total_copy(1).wait_recv()

    grad_score_ref[...] = total_buf[...]

    def dense_sent(i, carry):
        to, copy = dense_copy(i)

        @pl.when(to != node)
        def _():
            copy.wait_send()

        return carry

    lax.fori_loop(0, targets, dense_sent, 0)
    ids_copy().wait_send()
    for g in range(2):
        for d in range(1, n):
            line_push(g, d).wait_send()
        for s in range(1, half_ring + 1):
            for way in range(2):
                ring_copy(g, way, s, False).wait_send()
    for f in range(chunks):
        pick_copy(f).wait_send()
    for f in range(feats):
        for s in range(1, half_chip + 1):
            for way in range(2):
                chip_copy(f, way, s, False).wait_send()
    for d in range(1, ny):
        sum_copy(d, chip).wait_send()


def on_device(n, ny, grad_out, route_score, expert_routes, expert_count, gate_pre, up_pre, w_down):
    tokens, features = grad_out.shape
    experts, cap = expert_routes.shape
    hidden = gate_pre.shape[2]
    feats = features // LANES
    chunks = feats + 1
    slots = experts * cap
    nodes = 2 * n * n
    targets = 2 * n
    half_ring, half_chip = max(n // 2, 1), max(ny // 2, 1)
    bf16, f32 = jnp.bfloat16, jnp.float32
    dma = pltpu.SemaphoreType.DMA
    vmem = pl.BlockSpec(memory_space=pltpu.VMEM)
    hbm = pl.BlockSpec(memory_space=pl.ANY)
    grad_gate, grad_up, score = pl.pallas_call(
        functools.partial(kernel, n, ny),
        out_shape=(
            jax.ShapeDtypeStruct(gate_pre.shape, bf16),
            jax.ShapeDtypeStruct(gate_pre.shape, bf16),
            jax.ShapeDtypeStruct((2, LANES), f32),
        ),
        in_specs=[vmem, vmem, vmem, pl.BlockSpec(memory_space=pltpu.SMEM), hbm, hbm, hbm],
        out_specs=(vmem, vmem, vmem),
        scratch_shapes=[
            pltpu.VMEM((n, chunks, n, tokens, LANES), bf16),
            pltpu.VMEM((n, 2 * slots, n * tokens), bf16),
            pltpu.VMEM((2, experts, cap), jnp.int32),
            pltpu.VMEM((chunks, experts, cap, LANES), bf16),
            pltpu.VMEM((chunks, experts, cap, LANES), bf16),
            pltpu.VMEM((chunks, experts, cap, LANES), bf16),
            pltpu.VMEM((ny, feats, experts, cap, LANES), bf16),
            pltpu.VMEM(gate_pre.shape, bf16),
            pltpu.VMEM(up_pre.shape, bf16),
            pltpu.VMEM(w_down.shape, bf16),
            pltpu.VMEM((experts, cap, hidden), f32),
            pltpu.VMEM((slots, 2 * LANES), bf16),
            pltpu.VMEM((ny, slots // LANES, LANES), f32),
            pltpu.VMEM((targets, 2, LANES), f32),
            pltpu.VMEM((nodes, 2, LANES), f32),
            pltpu.VMEM((2, LANES), f32),
            dma((3,)),
            dma,
            dma,
            dma((2, n)),
            dma((2, n)),
            dma((2, 2, half_ring)),
            dma((2, 2, half_ring)),
            dma((chunks,)),
            dma((chunks,)),
            dma((feats, 2, half_chip)),
            dma((feats, 2, half_chip)),
            dma((ny,)),
            dma((ny,)),
            dma((targets,)),
            dma,
            dma((ny,)),
            dma,
        ],
        compiler_params=pltpu.CompilerParams(
            collective_id=0, has_side_effects=True, vmem_limit_bytes=40 * 1024 * 1024
        ),
        name="expert_backward",
    )(grad_out, route_score, expert_routes, expert_count, gate_pre, up_pre, w_down)
    return grad_gate, grad_up, score.reshape(tokens, -1)


def solution(mesh):
    ny = mesh.shape["chip"]
    n = 1
    while 2 * n * n < mesh.shape["node"]:
        n *= 2
    placed = (
        P("node", "chip"),
        P("node", None),
        P("node", None),
        P("node"),
        P("node", None, "chip"),
        P("node", None, "chip"),
        P("node", "chip", None),
    )
    return jax.shard_map(
        functools.partial(on_device, n, ny),
        mesh=mesh,
        in_specs=placed,
        out_specs=(P("node", None, "chip"), P("node", None, "chip"), P("node", None)),
        check_vma=False,
    )
```

time: 422 us -> 123 us (0.29)
  waiting for transfers between devices: 318 us -> 0 us
  Pallas kernels: 0 us -> 113 us
  blocking collectives: 60.5 us -> 0 us
  between operations: 13.9 us -> 0.65 us
  local copies, waits for them, and re-layouts: 15.9 us -> 8.32 us
  other arithmetic: 5.87 us -> 0 us
    reduce_scatter x1 -> x0, waiting for transfers between devices: 208 us -> none  [on_device(): lax.psum_scatter(flat_term.reshape(total_tokens, top_count), 'node', scat...]
    pallas_call x0 -> x1, Pallas kernels: none -> 113 us  [on_device(): pl.pallas_call(functools.partial(kernel, n, ny), out_shape=(jax.ShapeDtyp...]
    all_gather x2 -> x0, waiting for transfers between devices: 110 us -> none  [the longest x1 107 us: on_device(): lax.all_gather(grad_out, 'node', axis=0, tiled=True)]
    all_gather x1 -> x0, blocking collectives: 48.5 us -> none  [on_device(): lax.all_gather(route_score, 'node', axis=0, tiled=True)]
    psum x1 -> x0, blocking collectives: 12 us -> none  [on_device(): slot_total = lax.psum(partial_slot, 'chip')]
    gather x2 -> x0, local copies, waits for them, and re-layouts: 9.28 us -> none  [the longest x1 4.71 us: on_device(): gathered_rows[token_ids]]
  transfers between devices with their start and end apart: 3 -> 0, of which waited for: 3 -> 0; matrix products, arithmetic and copies ran while one was open for 2% -> 0% of each run, Pallas kernels for 0% -> 0%
where the time goes in v1:
time: 123 us; the launch traced here: 122 us
  Pallas kernels  113 us (92%)
  local copies, waits for them, and re-layouts  8.32 us (7%)
    pallas_call x1, Pallas kernels, on_device(): pl.pallas_call(functools.partial(kernel, n, ny), out_shape=(jax.ShapeDtyp...  113 us
    unnamed x16, local copies, waits for them, and re-layouts  8.24 us

profile of v1, /device:TPU:1, one launch (start us, length us, event | category | flops | bytes accessed | tf_op | source)
XLA Modules:
  0.0 122.4 jit_solution(15767966348447537480)
XLA Ops:
  0.6 0.8 copy.12.score_ref
  1.4 0.0 copy-start
  1.4 1.6 %copy-done = bf16[2,128,4096]{2,1,0:T(8,128)(2,1)S(1)} copy-done((bf16[2,128,4096]{2,1,0:T(8,128)(2,1)S(1)}, bf16[2,128,4096]{2,1,0:T(8,128)(2,1)}, u32[]{:S(2)}) %copy-start) | copy-done | bytes 2097176
  3.0 0.0 copy-start.1
  3.0 0.9 copy-done.1
  3.9 0.0 copy-start.2
  3.9 0.9 copy-done.2
  4.8 0.0 copy-start.3
  4.8 0.8 copy-done.3
  5.6 0.0 copy-start.4
  5.6 0.7 copy-done.4
  6.2 0.0 copy-start.5
  6.2 0.7 copy-done.5
  6.9 113.5 %expert_backward.1 = (bf16[2,256,128]{2,1,0:T(8,128)(2,1)S(1)}, bf16[2,256,128]{2,1,0:T(8,128)(2,1)S(1)}, f32[2,128]{1,0:T(2,128)S(1)}) custom-call(bf16[32,512]{1,0:T(8,128)(2,1)S(1)} %copy-done.3, bf16[32,8]{1,0:T(8,128)(2,1)S(1)} %copy.12.score_ref, s32[2,256]{1,0:T(2,128)S(1)} %copy-done.4, s32[2]{0:T(128)S(1)} %copy-done.5, ...), custom_call_target="tpu_custom_call" | custom-call | tf_op jit(solution)/shard_map/expert_backward/pallas_call | solution.py:472
  120.4 0.1 reshape.9
  120.4 0.7 copy.13
  121.1 0.7 copy.16
  121.8 0.7 copy.17
Async XLA Ops:
  1.4 1.6 %copy-start = (bf16[2,128,4096]{2,1,0:T(8,128)(2,1)S(1)}, bf16[2,128,4096]{2,1,0:T(8,128)(2,1)}, u32[]{:S(2)}) copy-start(bf16[2,128,4096]{2,1,0:T(8,128)(2,1)} %w_hbm.1) | copy-start | bytes 6291460
  3.0 0.9 copy-start.1
  3.9 0.9 copy-start.2
  4.8 0.8 copy-start.3
  5.6 0.7 copy-start.4
  6.2 0.7 copy-start.5

commit v2 on v1

--- a/solution.py
+++ b/solution.py
@@ -33,16 +33,19 @@
 def kernel(
     n,
     ny,
-    grad_ref,
+    grad_hbm,
     score_ref,
-    routes_ref,
-    count_ref,
+    routes_hbm,
+    count_hbm,
     gate_hbm,
     up_hbm,
     w_hbm,
     grad_gate_ref,
     grad_up_ref,
     grad_score_ref,
+    grad_ref,
+    routes_ref,
+    count_ref,
     table,
     onehot,
     ids,
@@ -58,12 +61,16 @@
     sums,
     dense_send,
     dense_recv,
-    total_buf,
+    totals,
     in_sem,
     ids_send_sem,
     ids_recv_sem,
     line_send,
     line_recv,
+    slab_send,
+    slab_recv,
+    wide_send,
+    wide_recv,
     ring_send,
     ring_recv,
     pick_send_sem,
@@ -77,15 +84,24 @@
     total_send,
     total_recv,
 ):
-    chunks = table.shape[1]
-    feats = chunks - 1
+    units = table.shape[1]
     tokens = table.shape[3]
     experts, cap = routes_ref.shape
     slots = experts * cap
     width = n * tokens
     half_ring, half_chip = n // 2, ny // 2
     nbits = bits_of(n)
-    groups = ((0, 1), (1, chunks))
+    feats = w_buf.shape[2] // (ny * LANES)
+    rounds = feats - 1
+    scores, slices = rounds, rounds + 1
+    apart = [0]
+    for d in range(1, half_chip):
+        apart += [d, -d]
+    apart += [half_chip]
+    pushes = ((0, 1), (1, slices + 1))
+    rings = [(1, rounds), (scores, slices + 1)]
+    for lo in range(slices + 1, max(units - 1, slices + 2), 2):
+        rings.append((lo, units if lo + 3 >= units else lo + 2))
 
     node = lax.axis_index("node")
     chip = lax.axis_index("chip")
@@ -105,59 +121,108 @@
         return lax.rem(line + d, n)
 
     loads = [
-        pltpu.make_async_copy(w_hbm, w_buf, in_sem.at[0]),
-        pltpu.make_async_copy(gate_hbm, gate_buf, in_sem.at[1]),
-        pltpu.make_async_copy(up_hbm, up_buf, in_sem.at[2]),
+        pltpu.make_async_copy(src, dst, in_sem.at[i])
+        for i, (src, dst) in enumerate(
+            (
+                (grad_hbm, grad_ref),
+                (routes_hbm, routes_ref),
+                (count_hbm, count_ref),
+                (w_hbm, w_buf),
+                (gate_hbm, gate_buf),
+                (up_hbm, up_buf),
+            )
+        )
     ]
     for load in loads:
         load.start()
-    for f in range(feats):
+
+    barrier = pltpu.get_barrier_semaphore()
+    greeted = [(sibling, chip)]
+    greeted += [(node_at(ring, line_peer(d)), chip) for d in range(1, n)]
+    greeted += [(node_at(lax.rem(ring + d, n), line), chip) for d in range(1, n)]
+    greeted += [(node, lax.rem(chip + d, ny)) for d in range(1, ny)]
+    for peer in greeted:
+        pl.semaphore_signal(
+            barrier, inc=1, device_id=peer, device_id_type=pl.DeviceIdType.MESH
+        )
+
+    for load in loads[:3]:
+        load.wait()
+    for f in range(rounds):
         table[ring, f, line] = grad_ref[:, f * LANES : (f + 1) * LANES]
+    table[ring, slices, line] = grad_ref[:, rounds * LANES : feats * LANES]
+    tops = score_ref.shape[0]
     padded = jnp.concatenate(
-        [
-            score_ref[...].astype(jnp.float32),
-            jnp.zeros((tokens, LANES - score_ref.shape[1]), jnp.float32),
-        ],
-        axis=1,
+        [score_ref[...].astype(jnp.float32), jnp.zeros((tops, LANES - tokens), jnp.float32)], axis=1
     )
-    table[ring, feats, line] = padded.astype(jnp.bfloat16)
+    padded = jnp.concatenate([padded, jnp.zeros((LANES - tops, LANES), jnp.float32)], axis=0)
+    table[ring, scores, line] = jnp.transpose(padded)[:tokens].astype(jnp.bfloat16)
     slot_lane = lax.broadcasted_iota(jnp.int32, (1, cap), 1)
     for e in range(experts):
         ids[0, e : e + 1, :] = jnp.where(
             slot_lane < count_ref[e], routes_ref[e : e + 1, :], -1
         )
-
-    barrier = pltpu.get_barrier_semaphore()
-    greeted = [(sibling, chip)]
-    greeted += [(node_at(ring, line_peer(d)), chip) for d in range(1, n)]
-    greeted += [(node_at(lax.rem(ring + d, n), line), chip) for d in sorted({1, n - 1})]
-    greeted += [(node, lax.rem(chip + d, ny)) for d in range(1, ny)]
-    for peer in greeted:
-        pl.semaphore_signal(
-            barrier, inc=1, device_id=peer, device_id_type=pl.DeviceIdType.MESH
-        )
     pl.semaphore_wait(barrier, len(greeted))
 
     def ids_copy():
         return remote(ids.at[0], ids.at[1], ids_send_sem, ids_recv_sem, sibling, chip)
 
+    far_first = sorted(range(1, n), key=lambda d: -min(d, n - d))
+
     def line_push(g, d):
-        lo, hi = groups[g]
+        lo, hi = pushes[g]
         block = table.at[ring, lo:hi, line]
         return remote(
             block, block, line_send.at[g, d], line_recv.at[g, line], node_at(ring, line_peer(d)), chip
         )
 
-    def line_arrival(g, d):
-        lo, hi = groups[g]
-        peer = line_peer(d)
-        block = table.at[ring, lo:hi, peer]
+    def line_start(g):
+        for d in far_first:
+            line_push(g, d).start()
+
+    def line_wait(g):
+        lo, hi = pushes[g]
+        for d in range(1, n):
+            peer = line_peer(d)
+            block = table.at[ring, lo:hi, peer]
+            remote(
+                block, block, line_send.at[g, d], line_recv.at[g, peer], node_at(ring, peer), chip
+            ).wait_recv()
+
+    def apart_chip(i):
+        return lax.rem(chip + apart[i] + ny, ny)
+
+    def slab_copy(i, arrival):
+        back_i = i if apart[i] == half_chip else apart.index(-apart[i])
+        mine = table.at[ring, slices]
+        if arrival:
+            block = table.at[ring, slices + i]
+            return remote(block, block, slab_send.at[i], slab_recv.at[i], node, apart_chip(i))
+        there = table.at[ring, slices + back_i]
+        return remote(mine, there, slab_send.at[i], slab_recv.at[back_i], node, apart_chip(i))
+
+    def slab_wait(*which):
+        for i in which:
+            if i < ny:
+                slab_copy(i, True).wait_recv()
+
+    def wide_push(d):
+        block = table.at[ring, 0]
+        peer = lax.rem(ring + d, n)
         return remote(
-            block, block, line_send.at[g, d], line_recv.at[g, peer], node_at(ring, peer), chip
-        )
+            block, block, wide_send.at[d], wide_recv.at[ring], node_at(peer, line), chip
+        )
+
+    def wide_wait():
+        for d in range(1, n):
+            peer = lax.rem(ring + d, n)
+            block = table.at[peer, 0]
+            remote(
+                block, block, wide_send.at[d], wide_recv.at[peer], node_at(peer, line), chip
+            ).wait_recv()
 
     def ring_block(g, way, s, pos):
-        lo, hi = groups[g]
+        lo, hi = rings[g]
         if s < half_ring:
             return table.at[pos, lo:hi]
         return table.at[pos, lo:hi, pl.ds(way * half_ring, half_ring)]
@@ -171,12 +236,16 @@
         return remote(block, block, ring_send.at[g, way, s - 1], ring_recv.at[g, way, s - 1], to, chip)
 
     def ring_start(g, s):
-        for way in range(2):
-            ring_copy(g, way, s, False).start()
-
-    def ring_wait(g, s):
-        for way in range(2):
-            ring_copy(g, way, s, True).wait_recv()
+        if g < len(rings):
+            for way in range(2):
+                ring_copy(g, way, s, False).start()
+
+    def ring_go(g, s):
+        if g < len(rings) and s <= half_ring:
+            for way in range(2):
+                ring_copy(g, way, s, True).wait_recv()
+            if s < half_ring:
+                ring_start(g, s + 1)
 
     def chip_copy(f, way, s, arrival):
         step = 1 if way == 0 else ny - 1
@@ -190,9 +259,12 @@
         for way in range(2):
             chip_copy(f, way, s, False).start()
 
-    def chip_wait(f, s):
-        for way in range(2):
-            chip_copy(f, way, s, True).wait_recv()
+    def chip_go(f, s):
+        if s <= half_chip:
+            for way in range(2):
+                chip_copy(f, way, s, True).wait_recv()
+            if s < half_chip:
+                chip_start(f, s + 1)
 
     def pick_copy(f):
         return remote(
@@ -258,9 +330,9 @@
             pick_copy(f).start()
         select(lo, hi, 0, pick_own)
 
-    def merge(f):
-        pick_copy(f).wait_recv()
-        picked[chip, f] = pick_own[f] + pick_recv[f]
+    def merge(unit, owner, f):
+        pick_copy(unit).wait_recv()
+        picked[owner, f] = pick_own[unit] + pick_recv[unit]
 
     def multiply(f, first):
         def body(e, carry):
@@ -278,55 +350,86 @@
 
         lax.fori_loop(0, experts, body, 0)
 
+    def ring_picks(g):
+        if g < len(rings):
+            lo, hi = rings[g]
+            for first in range(lo, hi, 2):
+                send_picks(first, min(first + 2, hi))
+
+    line_start(0)
     ids_copy().start()
-    for g in range(2):
-        for d in range(1, n):
-            line_push(g, d).start()
+    line_start(1)
     build_onehot(0)
-    for d in range(1, n):
-        line_arrival(0, d).wait_recv()
-    ring_start(0, 1)
+    line_wait(0)
+    for d in far_first:
+        wide_push(d).start()
     ids_copy().wait_recv()
     build_onehot(1)
-    for s in range(1, half_ring):
-        ring_wait(0, s)
-        ring_start(0, s + 1)
-    for d in range(1, n):
-        line_arrival(1, d).wait_recv()
+    line_wait(1)
+    ring_start(0, 1)
+    for i in range(1, ny):
+        slab_copy(i, False).start()
     ring_start(1, 1)
-    ring_wait(0, half_ring)
+    build_low_hot()
+    ring_go(0, 1)
+    slab_wait(1, 2)
+    ring_start(2, 1)
+    wide_wait()
     send_picks(0, 1)
-    build_low_hot()
-    merge(0)
+    ring_go(1, 1)
+    ring_go(0, 2)
+    slab_wait(3, 4)
+    ring_start(3, 1)
+    merge(0, chip, 0)
     chip_start(0, 1)
-    for load in loads:
+    ring_go(2, 1)
+    ring_go(1, 2)
+    slab_wait(5, 6, 7)
+    ring_start(4, 1)
+    ring_go(0, 3)
+    chip_go(0, 1)
+    ring_go(3, 1)
+    ring_go(2, 2)
+    ring_go(1, 3)
+    ring_go(0, 4)
+    ring_picks(0)
+    chip_go(0, 2)
+    for f in range(1, rounds):
+        merge(f, chip, f)
+        chip_start(f, 1)
+    ring_go(4, 1)
+    ring_go(3, 2)
+    ring_go(2, 3)
+    ring_go(1, 4)
+    ring_picks(1)
+    chip_go(0, 3)
+    for load in loads[3:]:
         load.wait()
-    for s in range(1, half_ring):
-        ring_wait(1, s)
-        ring_start(1, s + 1)
-        if s < half_chip:
-            chip_wait(0, s)
-            chip_start(0, s + 1)
-    ring_wait(1, half_ring)
-    for lo in range(1, feats, 2):
-        send_picks(lo, lo + 2)
-        for f in range(lo, min(lo + 2, feats)):
-            merge(f)
-            chip_start(f, 1)
-    for s in range(half_ring, half_chip):
-        chip_wait(0, s)
-        chip_start(0, s + 1)
-    merge_scores = feats
-    pick_copy(merge_scores).wait_recv()
-    chip_wait(0, half_chip)
+    ring_go(4, 2)
+    ring_go(3, 3)
+    ring_go(2, 4)
+    chip_go(1, 1)
+    chip_go(2, 1)
+    ring_picks(2)
+    chip_go(0, 4)
+    ring_go(4, 3)
+    ring_go(3, 4)
+    chip_go(1, 2)
+    chip_go(2, 2)
+    ring_picks(3)
     multiply(0, True)
-    for s in range(1, half_chip):
-        for f in range(1, feats):
-            chip_wait(f, s)
-            chip_start(f, s + 1)
-    for f in range(1, feats):
-        chip_wait(f, half_chip)
-        multiply(f, False)
+    ring_go(4, 4)
+    chip_go(1, 3)
+    chip_go(2, 3)
+    ring_picks(4)
+    for i in range(ny):
+        merge(slices + i, apart_chip(i), rounds)
+    multiply(rounds, False)
+    pick_copy(scores).wait_recv()
+    chip_go(1, 4)
+    multiply(1, False)
+    chip_go(2, 4)
+    multiply(2, False)
 
     for e in range(experts):
         for b in range(cap // LANES):
@@ -339,10 +442,10 @@
             row = ids[0, e : e + 1, b * LANES : (b + 1) * LANES]
             place = jnp.transpose(jnp.broadcast_to(row, (LANES, LANES))) & ((1 << TOP_BITS) - 1)
             lane = lax.broadcasted_iota(jnp.int32, (LANES, LANES), 1)
-            scores = pick_own[feats, e, rows, :].astype(jnp.float32) + pick_recv[
-                feats, e, rows, :
+            spread = pick_own[scores, e, rows, :].astype(jnp.float32) + pick_recv[
+                scores, e, rows, :
             ].astype(jnp.float32)
-            weight = jnp.sum(jnp.where(place == lane, scores, 0.0), axis=1, keepdims=True)
+            weight = jnp.sum(jnp.where(place == lane, spread, 0.0), axis=1, keepdims=True)
             product = silu * u * bk
             at = e * (cap // LANES) + b
             sums[chip, at : at + 1, :] = jnp.sum(jnp.transpose(product), axis=0, keepdims=True)
@@ -372,7 +475,7 @@
             row_z = (row_node >> 1) & (n - 1)
             row_x = row_node >> (1 + nbits)
             row_target = jnp.where(
-                ((row_z - row_x) & (n - 1)) == chip, row_x * 2 + (row_node & 1), -1
+                ((row_z - z) & (n - 1)) == chip, row_x * 2 + (row_node & 1), -1
             )
             target = lax.broadcasted_iota(jnp.int32, (targets, LANES), 0)
             pieces.append(jnp.where(row_target == target, full[at : at + 1, :], 0.0))
@@ -386,73 +489,68 @@
         dense_send[i, 0:1, :] = dense[i : i + 1, :LANES]
         dense_send[i, 1:2, :] = dense[i : i + 1, LANES:]
 
-    def dense_copy(i):
-        at_x = i // 2
-        at_z = lax.rem(at_x + chip, n)
-        to = (at_x * n + at_z) * 2 + lax.rem(i, 2)
-        return to, remote(
-            dense_send.at[i], dense_recv.at[node], dense_send_sem.at[i], dense_recv_sem, to, chip
-        )
-
-    def dense_start(i, carry):
-        to, copy = dense_copy(i)
-
-        @pl.when(to != node)
-        def _():
-            copy.start()
-
-        return carry
-
-    lax.fori_loop(0, targets, dense_start, 0)
-    owner = lax.rem(z - x + n, n) == chip
-
-    def total_copy(d):
+    mine = 2 * x + core
+
+    def dense_node(i, shift):
+        return ((i // 2) * n + lax.rem(z + shift, n)) * 2 + lax.rem(i, 2)
+
+    def dense_copy(i, slot, to):
         return remote(
-            total_buf, total_buf, total_send.at[d], total_recv, node, lax.rem(chip + d, ny)
-        )
-
-    @pl.when(owner)
+            dense_send.at[i], dense_recv.at[slot], dense_send_sem.at[i], dense_recv_sem.at[slot], to, chip
+        )
+
+    def each_target(act, shift):
+        def body(i, carry):
+            to = dense_node(i, shift)
+
+            @pl.when(to != node)
+            def _():
+                act(i, to)
+
+            return carry
+
+        lax.fori_loop(0, targets, body, 0)
+
+    each_target(lambda i, to: dense_copy(i, mine, to).start(), chip)
+
+    @pl.when(chip == 0)
     def _():
-        dense_recv[node] = dense_send[2 * x + core]
-        others = dense_recv.at[pl.ds(0, dense_recv.shape[0] - 1)]
-        pltpu.make_async_copy(others, others, dense_recv_sem).wait()
-        total_buf[...] = jnp.sum(dense_recv[...], axis=0)
-        for d in range(1, ny):
-            total_copy(d).start()
-        for d in range(1, ny):
-            total_copy(d).wait_send()
-
-    @pl.when(jnp.logical_not(owner))
-    def _():
-        total_copy(1).wait_recv()
-
-    grad_score_ref[...] = total_buf[...]
-
-    def dense_sent(i, carry):
-        to, copy = dense_copy(i)
-
-        @pl.when(to != node)
-        def _():
-            copy.wait_send()
-
-        return carry
-
-    lax.fori_loop(0, targets, dense_sent, 0)
+        dense_recv[mine] = dense_send[mine]
+
+    each_target(lambda i, to: dense_copy(i, i, to).wait_recv(), n - chip)
+    totals[chip] = jnp.sum(dense_recv[...], axis=0)
+
+    def total_copy(d, slot):
+        return remote(
+            totals.at[slot], totals.at[slot], total_send.at[d], total_recv.at[slot], node, lax.rem(chip + d, ny)
+        )
+
+    for d in range(1, ny):
+        total_copy(d, chip).start()
+    for d in range(1, ny):
+        total_copy(d, lax.rem(chip + d, ny)).wait_recv()
+    grad_score_ref[...] = jnp.sum(totals[...], axis=0)
+
+    each_target(lambda i, to: dense_copy(i, mine, to).wait_send(), chip)
     ids_copy().wait_send()
-    for g in range(2):
-        for d in range(1, n):
+    for d in range(1, n):
+        wide_push(d).wait_send()
+        for g in range(2):
             line_push(g, d).wait_send()
+    for g in range(len(rings)):
         for s in range(1, half_ring + 1):
             for way in range(2):
                 ring_copy(g, way, s, False).wait_send()
-    for f in range(chunks):
-        pick_copy(f).wait_send()
-    for f in range(feats):
+    for u in range(units):
+        pick_copy(u).wait_send()
+    for f in range(rounds):
         for s in range(1, half_chip + 1):
             for way in range(2):
                 chip_copy(f, way, s, False).wait_send()
     for d in range(1, ny):
+        slab_copy(d, False).wait_send()
         sum_copy(d, chip).wait_send()
+        total_copy(d, chip).wait_send()
 
 
 def on_device(n, ny, grad_out, route_score, expert_routes, expert_count, gate_pre, up_pre, w_down):
@@ -460,15 +558,14 @@
     experts, cap = expert_routes.shape
     hidden = gate_pre.shape[2]
     feats = features // LANES
-    chunks = feats + 1
+    units = feats + ny
     slots = experts * cap
-    nodes = 2 * n * n
     targets = 2 * n
     half_ring, half_chip = max(n // 2, 1), max(ny // 2, 1)
     bf16, f32 = jnp.bfloat16, jnp.float32
     dma = pltpu.SemaphoreType.DMA
     vmem = pl.BlockSpec(memory_space=pltpu.VMEM)
-    hbm = pl.BlockSpec(memory_space=pl.ANY)
+    hbm = pl.BlockSpec(memory_space=pltpu.HBM)
     grad_gate, grad_up, score = pl.pallas_call(
         functools.partial(kernel, n, ny),
         out_shape=(
@@ -476,15 +573,18 @@
             jax.ShapeDtypeStruct(gate_pre.shape, bf16),
             jax.ShapeDtypeStruct((2, LANES), f32),
         ),
-        in_specs=[vmem, vmem, vmem, pl.BlockSpec(memory_space=pltpu.SMEM), hbm, hbm, hbm],
+        in_specs=[hbm, vmem, hbm, hbm, hbm, hbm, hbm],
         out_specs=(vmem, vmem, vmem),
         scratch_shapes=[
-            pltpu.VMEM((n, chunks, n, tokens, LANES), bf16),
+            pltpu.VMEM(grad_out.shape, bf16),
+            pltpu.VMEM(expert_routes.shape, jnp.int32),
+            pltpu.SMEM(expert_count.shape, jnp.int32),
+            pltpu.VMEM((n, units, n, tokens, LANES), bf16),
             pltpu.VMEM((n, 2 * slots, n * tokens), bf16),
             pltpu.VMEM((2, experts, cap), jnp.int32),
-            pltpu.VMEM((chunks, experts, cap, LANES), bf16),
-            pltpu.VMEM((chunks, experts, cap, LANES), bf16),
-            pltpu.VMEM((chunks, experts, cap, LANES), bf16),
+            pltpu.VMEM((units, experts, cap, LANES), bf16),
+            pltpu.VMEM((units, experts, cap, LANES), bf16),
+            pltpu.VMEM((units, experts, cap, LANES), bf16),
             pltpu.VMEM((ny, feats, experts, cap, LANES), bf16),
             pltpu.VMEM(gate_pre.shape, bf16),
             pltpu.VMEM(up_pre.shape, bf16),
@@ -493,31 +593,35 @@
             pltpu.VMEM((slots, 2 * LANES), bf16),
             pltpu.VMEM((ny, slots // LANES, LANES), f32),
             pltpu.VMEM((targets, 2, LANES), f32),
-            pltpu.VMEM((nodes, 2, LANES), f32),
-            pltpu.VMEM((2, LANES), f32),
-            dma((3,)),
+            pltpu.VMEM((targets, 2, LANES), f32),
+            pltpu.VMEM((ny, 2, LANES), f32),
+            dma((6,)),
             dma,
             dma,
             dma((2, n)),
             dma((2, n)),
-            dma((2, 2, half_ring)),
-            dma((2, 2, half_ring)),
-            dma((chunks,)),
-            dma((chunks,)),
-            dma((feats, 2, half_chip)),
-            dma((feats, 2, half_chip)),
+            dma((ny,)),
+            dma((ny,)),
+            dma((n,)),
+            dma((n,)),
+            dma((units // 2, 2, half_ring)),
+            dma((units // 2, 2, half_ring)),
+            dma((units,)),
+            dma((units,)),
+            dma((feats - 1, 2, half_chip)),
+            dma((feats - 1, 2, half_chip)),
             dma((ny,)),
             dma((ny,)),
             dma((targets,)),
-            dma,
+            dma((targets,)),
             dma((ny,)),
-            dma,
+            dma((ny,)),
         ],
         compiler_params=pltpu.CompilerParams(
-            collective_id=0, has_side_effects=True, vmem_limit_bytes=40 * 1024 * 1024
+            collective_id=0, has_side_effects=True, vmem_limit_bytes=63 * 1024 * 1024
         ),
         name="expert_backward",
-    )(grad_out, route_score, expert_routes, expert_count, gate_pre, up_pre, w_down)
+    )(grad_out, route_score.T, expert_routes, expert_count, gate_pre, up_pre, w_down)
     return grad_gate, grad_up, score.reshape(tokens, -1)
 
 

time: 123 us -> 110 us (0.89)
  Pallas kernels: 113 us -> 104 us
  local copies, waits for them, and re-layouts: 8.32 us -> 4.56 us
    pallas_call x1, Pallas kernels: 113 us -> 104 us  [on_device(): pl.pallas_call(functools.partial(kernel, n, ny), out_shape=(jax.ShapeDtyp...]
    unnamed x16 -> x3, local copies, waits for them, and re-layouts: 8.24 us -> 3.81 us
where the time goes in v2:
time: 110 us
  Pallas kernels  104 us (95%)
  local copies, waits for them, and re-layouts  4.56 us (4%)
    pallas_call x1, Pallas kernels, on_device(): pl.pallas_call(functools.partial(kernel, n, ny), out_shape=(jax.ShapeDtyp...  104 us
    unnamed x3, local copies, waits for them, and re-layouts  3.81 us

profile of v2, /device:TPU:1, one launch (start us, length us, event | category | flops | bytes accessed | tf_op | source)
XLA Modules:
  0.0 109.6 jit_solution(3408828587445337141)
XLA Ops:
  0.6 104.4 %expert_backward.1 = (bf16[2,256,128]{2,1,0:T(8,128)(2,1)}, bf16[2,256,128]{2,1,0:T(8,128)(2,1)}, f32[2,128]{1,0:T(2,128)}) custom-call(bf16[32,512]{1,0:T(8,128)(2,1)} %grad_hbm.1, bf16[8,32]{1,0:T(8,128)(2,1)} %bitcast.1, s32[2,256]{1,0:T(2,128)} %routes_hbm.1, s32[2]{0:T(128)} %count_hbm.1, bf16[2,256,128]{2,1,0:T(8,128)(2,1)} %gate_hbm.1, ...), custom_call_target="tpu_custom_call" | custom-call | tf_op jit(solution)/shard_map/expert_backward/pallas_call | solution.py:569
  105.0 0.7 reshape.9
  105.8 0.7 copy.11
  106.5 1.6 %copy.14 = bf16[2,256,128]{2,1,0:T(8,128)(2,1)} copy(bf16[2,256,128]{2,1,0:T(8,128)(2,1)} %get-tuple-element.18) | data formatting | bytes 262144
  108.0 1.6 %copy.15 = bf16[2,256,128]{2,1,0:T(8,128)(2,1)} copy(bf16[2,256,128]{2,1,0:T(8,128)(2,1)} %get-tuple-element.19) | data formatting | bytes 262144

commit v3 on v2

--- a/solution.py
+++ b/solution.py
@@ -9,6 +9,7 @@
 
 LANES = 128
 TOP_BITS = 3
+NEAR = 1
 
 
 def bits_of(size):
@@ -17,6 +18,17 @@
 
 def dot_f32(a, b):
     return jnp.dot(a, b, preferred_element_type=jnp.float32)
+
+
+def near_steps(ny):
+    return max(min(NEAR, ny // 2 - 1), 0)
+
+
+def far_chips(ny):
+    apart = [0]
+    for d in range(near_steps(ny) + 1, ny // 2):
+        apart += [d, -d]
+    return apart + [ny // 2]
 
 
 def remote(src, dst, send, recv, node, chip):
@@ -94,14 +106,15 @@
     feats = w_buf.shape[2] // (ny * LANES)
     rounds = feats - 1
     scores, slices = rounds, rounds + 1
-    apart = [0]
-    for d in range(1, half_chip):
-        apart += [d, -d]
-    apart += [half_chip]
+    reach = near_steps(ny)
+    apart = far_chips(ny)
     pushes = ((0, 1), (1, slices + 1))
-    rings = [(1, rounds), (scores, slices + 1)]
+    rings = [(scores, slices + 1)]
     for lo in range(slices + 1, max(units - 1, slices + 2), 2):
         rings.append((lo, units if lo + 3 >= units else lo + 2))
+
+    def last_step(f):
+        return reach if f == rounds else half_chip
 
     node = lax.axis_index("node")
     chip = lax.axis_index("chip")
@@ -201,24 +214,32 @@
         there = table.at[ring, slices + back_i]
         return remote(mine, there, slab_send.at[i], slab_recv.at[back_i], node, apart_chip(i))
 
+    def slab_start():
+        for i in range(1, len(apart)):
+            slab_copy(i, False).start()
+
     def slab_wait(*which):
         for i in which:
-            if i < ny:
+            if i < len(apart):
                 slab_copy(i, True).wait_recv()
 
-    def wide_push(d):
-        block = table.at[ring, 0]
+    def wide_push(f, d):
+        block = table.at[ring, f]
         peer = lax.rem(ring + d, n)
         return remote(
-            block, block, wide_send.at[d], wide_recv.at[ring], node_at(peer, line), chip
-        )
-
-    def wide_wait():
+            block, block, wide_send.at[f, d], wide_recv.at[f, ring], node_at(peer, line), chip
+        )
+
+    def wide_start(f):
+        for d in far_first:
+            wide_push(f, d).start()
+
+    def wide_wait(f):
         for d in range(1, n):
             peer = lax.rem(ring + d, n)
-            block = table.at[peer, 0]
+            block = table.at[peer, f]
             remote(
-                block, block, wide_send.at[d], wide_recv.at[peer], node_at(peer, line), chip
+                block, block, wide_send.at[f, d], wide_recv.at[f, peer], node_at(peer, line), chip
             ).wait_recv()
 
     def ring_block(g, way, s, pos):
@@ -256,15 +277,15 @@
         return remote(block, block, chip_send.at[f, way, s - 1], chip_recv.at[f, way, s - 1], node, to)
 
     def chip_start(f, s):
-        for way in range(2):
-            chip_copy(f, way, s, False).start()
+        if s <= last_step(f):
+            for way in range(2):
+                chip_copy(f, way, s, False).start()
 
     def chip_go(f, s):
-        if s <= half_chip:
+        if s <= last_step(f):
             for way in range(2):
                 chip_copy(f, way, s, True).wait_recv()
-            if s < half_chip:
-                chip_start(f, s + 1)
+            chip_start(f, s + 1)
 
     def pick_copy(f):
         return remote(
@@ -311,6 +332,10 @@
                 ).astype(jnp.bfloat16)
 
     def select(lo, hi, side, out):
+        hi = min(hi, units)
+        if lo >= hi:
+            return
+
         def body(e, carry):
             first = pl.multiple_of((side * experts + e) * cap, cap)
             total = jnp.zeros((cap, (hi - lo) * LANES), jnp.float32)
@@ -324,17 +349,25 @@
 
         lax.fori_loop(0, experts, body, 0)
 
-    def send_picks(lo, hi):
+    def send_away(lo, hi):
         select(lo, hi, 1, pick_send)
-        for f in range(lo, hi):
+        for f in range(lo, min(hi, units)):
             pick_copy(f).start()
+
+    def pick_here(lo, hi):
         select(lo, hi, 0, pick_own)
 
-    def merge(unit, owner, f):
-        pick_copy(unit).wait_recv()
-        picked[owner, f] = pick_own[unit] + pick_recv[unit]
-
-    def multiply(f, first):
+    def merge(unit):
+        if unit < units:
+            pick_copy(unit).wait_recv()
+            far = unit >= slices
+            owner = apart_chip(unit - slices) if far else chip
+            f = rounds if far else unit
+            picked[owner, f] = pick_own[unit] + pick_recv[unit]
+            if unit <= slices:
+                chip_start(f, 1)
+
+    def multiply(f, first=False):
         def body(e, carry):
             total = jnp.zeros((cap, LANES), jnp.float32) if first else back[e]
             for y in range(ny):
@@ -350,86 +383,82 @@
 
         lax.fori_loop(0, experts, body, 0)
 
-    def ring_picks(g):
-        if g < len(rings):
-            lo, hi = rings[g]
-            for first in range(lo, hi, 2):
-                send_picks(first, min(first + 2, hi))
-
     line_start(0)
     ids_copy().start()
     line_start(1)
     build_onehot(0)
-    line_wait(0)
-    for d in far_first:
-        wide_push(d).start()
     ids_copy().wait_recv()
     build_onehot(1)
+    build_low_hot()
+    line_wait(0)
+    wide_start(0)
     line_wait(1)
+    slab_start()
+    wide_start(1)
+    wide_start(2)
     ring_start(0, 1)
-    for i in range(1, ny):
-        slab_copy(i, False).start()
+    slab_wait(1, 2)
     ring_start(1, 1)
-    build_low_hot()
+    wide_wait(0)
+    send_away(0, 1)
+    pick_here(0, 1)
+    merge(0)
+    wide_wait(1)
+    send_away(1, 2)
+    pick_here(1, 2)
+    merge(1)
+    chip_go(0, 1)
+    wide_wait(2)
+    slab_wait(3, 4, 5)
+    ring_start(2, 1)
+    send_away(2, 3)
+    chip_go(1, 1)
+    pick_here(2, 3)
     ring_go(0, 1)
-    slab_wait(1, 2)
-    ring_start(2, 1)
-    wide_wait()
-    send_picks(0, 1)
+    merge(2)
     ring_go(1, 1)
+    chip_go(0, 2)
+    ring_go(2, 1)
     ring_go(0, 2)
-    slab_wait(3, 4)
-    ring_start(3, 1)
-    merge(0, chip, 0)
-    chip_start(0, 1)
-    ring_go(2, 1)
+    chip_go(1, 2)
     ring_go(1, 2)
-    slab_wait(5, 6, 7)
-    ring_start(4, 1)
+    chip_go(2, 1)
+    ring_go(2, 2)
     ring_go(0, 3)
-    chip_go(0, 1)
-    ring_go(3, 1)
-    ring_go(2, 2)
+    chip_go(0, 3)
     ring_go(1, 3)
+    chip_go(1, 3)
+    ring_go(2, 3)
     ring_go(0, 4)
-    ring_picks(0)
-    chip_go(0, 2)
-    for f in range(1, rounds):
-        merge(f, chip, f)
-        chip_start(f, 1)
-    ring_go(4, 1)
-    ring_go(3, 2)
-    ring_go(2, 3)
+    send_away(3, 5)
     ring_go(1, 4)
-    ring_picks(1)
-    chip_go(0, 3)
+    pick_here(3, 5)
+    chip_go(2, 2)
+    send_away(5, 7)
+    merge(4)
+    pick_here(5, 7)
+    chip_go(0, 4)
+    ring_go(2, 4)
+    send_away(7, 9)
+    chip_go(1, 4)
+    pick_here(7, 9)
+    send_away(9, 10)
+    pick_here(9, 10)
+    chip_go(2, 3)
+    merge(5)
+    merge(6)
+    merge(7)
+    merge(8)
+    merge(9)
     for load in loads[3:]:
         load.wait()
-    ring_go(4, 2)
-    ring_go(3, 3)
-    ring_go(2, 4)
-    chip_go(1, 1)
-    chip_go(2, 1)
-    ring_picks(2)
-    chip_go(0, 4)
-    ring_go(4, 3)
-    ring_go(3, 4)
-    chip_go(1, 2)
-    chip_go(2, 2)
-    ring_picks(3)
     multiply(0, True)
-    ring_go(4, 4)
-    chip_go(1, 3)
-    chip_go(2, 3)
-    ring_picks(4)
-    for i in range(ny):
-        merge(slices + i, apart_chip(i), rounds)
-    multiply(rounds, False)
+    multiply(1)
     pick_copy(scores).wait_recv()
-    chip_go(1, 4)
-    multiply(1, False)
+    chip_go(3, 1)
+    multiply(rounds)
     chip_go(2, 4)
-    multiply(2, False)
+    multiply(2)
 
     for e in range(experts):
         for b in range(cap // LANES):
@@ -534,7 +563,8 @@
     each_target(lambda i, to: dense_copy(i, mine, to).wait_send(), chip)
     ids_copy().wait_send()
     for d in range(1, n):
-        wide_push(d).wait_send()
+        for f in range(rounds):
+            wide_push(f, d).wait_send()
         for g in range(2):
             line_push(g, d).wait_send()
     for g in range(len(rings)):
@@ -543,12 +573,13 @@
                 ring_copy(g, way, s, False).wait_send()
     for u in range(units):
         pick_copy(u).wait_send()
-    for f in range(rounds):
-        for s in range(1, half_chip + 1):
+    for f in range(feats):
+        for s in range(1, last_step(f) + 1):
             for way in range(2):
                 chip_copy(f, way, s, False).wait_send()
+    for i in range(1, len(apart)):
+        slab_copy(i, False).wait_send()
     for d in range(1, ny):
-        slab_copy(d, False).wait_send()
         sum_copy(d, chip).wait_send()
         total_copy(d, chip).wait_send()
 
@@ -558,7 +589,7 @@
     experts, cap = expert_routes.shape
     hidden = gate_pre.shape[2]
     feats = features // LANES
-    units = feats + ny
+    units = feats + len(far_chips(ny))
     slots = experts * cap
     targets = 2 * n
     half_ring, half_chip = max(n // 2, 1), max(ny // 2, 1)
@@ -600,16 +631,16 @@
             dma,
             dma((2, n)),
             dma((2, n)),
-            dma((ny,)),
-            dma((ny,)),
-            dma((n,)),
-            dma((n,)),
-            dma((units // 2, 2, half_ring)),
-            dma((units // 2, 2, half_ring)),
+            dma((len(far_chips(ny)),)),
+            dma((len(far_chips(ny)),)),
+            dma((feats - 1, n)),
+            dma((feats - 1, n)),
+            dma((4, 2, half_ring)),
+            dma((4, 2, half_ring)),
             dma((units,)),
             dma((units,)),
-            dma((feats - 1, 2, half_chip)),
-            dma((feats - 1, 2, half_chip)),
+            dma((feats, 2, half_chip)),
+            dma((feats, 2, half_chip)),
             dma((ny,)),
             dma((ny,)),
             dma((targets,)),

time: 110 us -> 103 us (0.936)
  Pallas kernels: 104 us -> 97.4 us
    pallas_call x1, Pallas kernels: 104 us -> 97.4 us  [on_device(): pl.pallas_call(functools.partial(kernel, n, ny), out_shape=(jax.ShapeDtyp...]
where the time goes in v3:
time: 103 us
  Pallas kernels  97.4 us (95%)
  local copies, waits for them, and re-layouts  4.56 us (4%)
    pallas_call x1, Pallas kernels, on_device(): pl.pallas_call(functools.partial(kernel, n, ny), out_shape=(jax.ShapeDtyp...  97.4 us
    unnamed x3, local copies, waits for them, and re-layouts  3.81 us

profile of v3, /device:TPU:1, one launch (start us, length us, event | category | flops | bytes accessed | tf_op | source)
XLA Modules:
  0.0 102.6 jit_solution(1638079243245551851)
XLA Ops:
  0.6 97.4 %expert_backward.1 = (bf16[2,256,128]{2,1,0:T(8,128)(2,1)}, bf16[2,256,128]{2,1,0:T(8,128)(2,1)}, f32[2,128]{1,0:T(2,128)}) custom-call(bf16[32,512]{1,0:T(8,128)(2,1)} %grad_hbm.1, bf16[8,32]{1,0:T(8,128)(2,1)} %bitcast.1, s32[2,256]{1,0:T(2,128)} %routes_hbm.1, s32[2]{0:T(128)} %count_hbm.1, bf16[2,256,128]{2,1,0:T(8,128)(2,1)} %gate_hbm.1, ...), custom_call_target="tpu_custom_call" | custom-call | tf_op jit(solution)/shard_map/expert_backward/pallas_call | solution.py:600
  98.1 0.7 reshape.9
  98.8 0.7 copy.11
  99.5 1.6 %copy.14 = bf16[2,256,128]{2,1,0:T(8,128)(2,1)} copy(bf16[2,256,128]{2,1,0:T(8,128)(2,1)} %get-tuple-element.18) | data formatting | bytes 262144
  101.1 1.6 %copy.15 = bf16[2,256,128]{2,1,0:T(8,128)(2,1)} copy(bf16[2,256,128]{2,1,0:T(8,128)(2,1)} %get-tuple-element.19) | data formatting | bytes 262144

commit v4 on v3

--- a/solution.py
+++ b/solution.py
@@ -29,6 +29,10 @@
     for d in range(near_steps(ny) + 1, ny // 2):
         apart += [d, -d]
     return apart + [ny // 2]
+
+
+def in_hbm(array):
+    return pltpu.with_memory_space_constraint(array, pltpu.HBM)
 
 
 def remote(src, dst, send, recv, node, chip):
@@ -460,14 +464,31 @@
     chip_go(2, 4)
     multiply(2)
 
+    def hidden_parts(e, rows):
+        g = gate_buf[e, rows, :].astype(jnp.float32)
+        u = up_buf[e, rows, :].astype(jnp.float32)
+        s = 1.0 / (1.0 + jnp.exp(-g))
+        return g, u, s, g * s
+
+    slot_rows = [slice(b * LANES, (b + 1) * LANES) for b in range(cap // LANES)]
     for e in range(experts):
-        for b in range(cap // LANES):
-            rows = slice(b * LANES, (b + 1) * LANES)
-            g = gate_buf[e, rows, :].astype(jnp.float32)
-            u = up_buf[e, rows, :].astype(jnp.float32)
-            bk = back[e, rows, :]
-            s = 1.0 / (1.0 + jnp.exp(-g))
-            silu = g * s
+        for b, rows in enumerate(slot_rows):
+            g, u, s, silu = hidden_parts(e, rows)
+            product = silu * u * back[e, rows, :]
+            at = e * (cap // LANES) + b
+            sums[chip, at : at + 1, :] = jnp.sum(jnp.transpose(product), axis=0, keepdims=True)
+
+    def sum_copy(d, slot):
+        return remote(
+            sums.at[slot], sums.at[slot], sum_send.at[d], sum_recv.at[slot], node, lax.rem(chip + d, ny)
+        )
+
+    for d in range(1, ny):
+        sum_copy(d, chip).start()
+
+    for e in range(experts):
+        for b, rows in enumerate(slot_rows):
+            g, u, s, silu = hidden_parts(e, rows)
             row = ids[0, e : e + 1, b * LANES : (b + 1) * LANES]
             place = jnp.transpose(jnp.broadcast_to(row, (LANES, LANES))) & ((1 << TOP_BITS) - 1)
             lane = lax.broadcasted_iota(jnp.int32, (LANES, LANES), 1)
@@ -475,20 +496,29 @@
                 scores, e, rows, :
             ].astype(jnp.float32)
             weight = jnp.sum(jnp.where(place == lane, spread, 0.0), axis=1, keepdims=True)
-            product = silu * u * bk
-            at = e * (cap // LANES) + b
-            sums[chip, at : at + 1, :] = jnp.sum(jnp.transpose(product), axis=0, keepdims=True)
-            scaled = weight * bk
+            scaled = weight * back[e, rows, :]
             grad_gate_ref[e, rows, :] = (scaled * u * (s * (1.0 + g * (1.0 - s)))).astype(jnp.bfloat16)
             grad_up_ref[e, rows, :] = (scaled * silu).astype(jnp.bfloat16)
 
-    def sum_copy(d, slot):
-        return remote(
-            sums.at[slot], sums.at[slot], sum_send.at[d], sum_recv.at[slot], node, lax.rem(chip + d, ny)
-        )
-
-    for d in range(1, ny):
-        sum_copy(d, chip).start()
+    ids_copy().wait_send()
+    for d in range(1, n):
+        for f in range(rounds):
+            wide_push(f, d).wait_send()
+        for g in range(2):
+            line_push(g, d).wait_send()
+    for g in range(len(rings)):
+        for s in range(1, half_ring + 1):
+            for way in range(2):
+                ring_copy(g, way, s, False).wait_send()
+    for u in range(units):
+        pick_copy(u).wait_send()
+    for f in range(feats):
+        for s in range(1, last_step(f) + 1):
+            for way in range(2):
+                chip_copy(f, way, s, False).wait_send()
+    for i in range(1, len(apart)):
+        slab_copy(i, False).wait_send()
+
     for d in range(1, ny):
         sum_copy(d, lax.rem(chip + d, ny)).wait_recv()
     full = sums[0]
@@ -546,6 +576,8 @@
     def _():
         dense_recv[mine] = dense_send[mine]
 
+    for d in range(1, ny):
+        sum_copy(d, chip).wait_send()
     each_target(lambda i, to: dense_copy(i, i, to).wait_recv(), n - chip)
     totals[chip] = jnp.sum(dense_recv[...], axis=0)
 
@@ -556,31 +588,11 @@
 
     for d in range(1, ny):
         total_copy(d, chip).start()
+    each_target(lambda i, to: dense_copy(i, mine, to).wait_send(), chip)
     for d in range(1, ny):
         total_copy(d, lax.rem(chip + d, ny)).wait_recv()
     grad_score_ref[...] = jnp.sum(totals[...], axis=0)
-
-    each_target(lambda i, to: dense_copy(i, mine, to).wait_send(), chip)
-    ids_copy().wait_send()
-    for d in range(1, n):
-        for f in range(rounds):
-            wide_push(f, d).wait_send()
-        for g in range(2):
-            line_push(g, d).wait_send()
-    for g in range(len(rings)):
-        for s in range(1, half_ring + 1):
-            for way in range(2):
-                ring_copy(g, way, s, False).wait_send()
-    for u in range(units):
-        pick_copy(u).wait_send()
-    for f in range(feats):
-        for s in range(1, last_step(f) + 1):
-            for way in range(2):
-                chip_copy(f, way, s, False).wait_send()
-    for i in range(1, len(apart)):
-        slab_copy(i, False).wait_send()
     for d in range(1, ny):
-        sum_copy(d, chip).wait_send()
         total_copy(d, chip).wait_send()
 
 
@@ -649,10 +661,18 @@
             dma((ny,)),
         ],
         compiler_params=pltpu.CompilerParams(
-            collective_id=0, has_side_effects=True, vmem_limit_bytes=63 * 1024 * 1024
+            collective_id=0, has_side_effects=True, vmem_limit_bytes=40 * 1024 * 1024
         ),
         name="expert_backward",
-    )(grad_out, route_score.T, expert_routes, expert_count, gate_pre, up_pre, w_down)
+    )(
+        in_hbm(grad_out),
+        route_score.T,
+        in_hbm(expert_routes),
+        in_hbm(expert_count),
+        in_hbm(gate_pre),
+        in_hbm(up_pre),
+        in_hbm(w_down),
+    )
     return grad_gate, grad_up, score.reshape(tokens, -1)
 
 

time: 103 us -> 99.2 us (0.963)
  local copies, waits for them, and re-layouts: 4.56 us -> 2.74 us
  Pallas kernels: 97.4 us -> 95.7 us
    pallas_call x1, Pallas kernels: 97.4 us -> 95.7 us  [on_device(): pl.pallas_call(functools.partial(kernel, n, ny), out_shape=(jax.ShapeDtyp...]
    unnamed x3 -> x5, local copies, waits for them, and re-layouts: 3.81 us -> 2.66 us
where the time goes in v4:
time: 99.2 us; the launch traced here: 99 us
  Pallas kernels  95.7 us (96%)
  local copies, waits for them, and re-layouts  2.74 us (3%)
    pallas_call x1, Pallas kernels, on_device(): pl.pallas_call(functools.partial(kernel, n, ny), out_shape=(jax.ShapeDtyp...  95.7 us
    unnamed x5, local copies, waits for them, and re-layouts  2.66 us

profile of v4, /device:TPU:1, one launch (start us, length us, event | category | flops | bytes accessed | tf_op | source)
XLA Modules:
  0.0 99.0 jit_solution(8632032962034443937)
XLA Ops:
  0.6 0.0 copy-start
  0.6 0.7 copy-done
  1.3 95.7 %expert_backward.1 = (bf16[2,256,128]{2,1,0:T(8,128)(2,1)S(1)}, bf16[2,256,128]{2,1,0:T(8,128)(2,1)S(1)}, f32[2,128]{1,0:T(2,128)S(1)}) custom-call(bf16[32,512]{1,0:T(8,128)(2,1)} %grad_hbm.1, bf16[8,32]{1,0:T(8,128)(2,1)S(1)} %bitcast.1, s32[2,256]{1,0:T(2,128)} %routes_hbm.1, s32[2]{0:T(128)} %count_hbm.1, bf16[2,256,128]{2,1,0:T(8,128)(2,1)} %gate_hbm.1, ...), custom_call_target="tpu_custom_call" | custom-call | tf_op jit(solution)/shard_map/expert_backward/pallas_call | solution.py:612
  97.0 0.1 reshape.9
  97.1 0.7 copy.11
  97.7 0.7 copy.14
  98.4 0.7 copy.15
Async XLA Ops:
  0.6 0.7 copy-start
